TPU v7x, 32 devices: a whole 2x2x4 slice. The times are simulated.
32 devices in a mesh: row: 4 (over z), col: 4 (over y, core), front: 2 (over x).
Axes of the slice: x: 2, y: 2, z: 4, core: 2. Of those that a mesh axis runs over, the one named last changes fastest.
Arguments:
- front: float32 [2, 12, 1024, 12, 1024], P('front', None, 'row', None, 'col')
- child_update: float32 [2, 2048, 2048], P('front', 'row', 'col'), may hold values from -6 to 6
- child_map: int32 [2, 2048], P('front'), may hold values from 0 to 12287, as said below
- pattern: int32 [2, 48, 48], P('front'), may hold values 0 or 1
Outputs:
- new_front: float32 [2, 12, 1024, 12, 1024], P('front', None, 'row', None, 'col')
Inputs may be any that keep to these rules, and one draw needn't show every extreme that they name: `child_map`: entries of one front are distinct. Each aligned run of 512 entries holds exactly 128 entries g with (g // 256) % 4 equal to each index of col.
All inputs are finite; a program needn't handle non-finite values. No bound on the sum of `pattern` on one device may be relied on, other than what follows from the above.
Results may differ from a plain program's by a relative error of at most 0.0001.
Values sent between devices are 32-bit elements; how exact they have to be, the bound alone decides.
A program may use at most 320 MiB of HBM per device.

v0:
```python
import jax
import jax.numpy as jnp
from jax import lax
from jax.sharding import PartitionSpec as P

PB = 4
PW = 1024


def broadcast(value, axis, source):
    kept = jnp.where(lax.axis_index(axis) == source, value, 0).astype(value.dtype)
    return lax.psum(kept, axis)


def per_device(front, child_update, child_map, pattern):
    rows_count = lax.axis_size("row")
    cols_count = lax.axis_size("col")
    row_place = lax.axis_index("row")
    col_place = lax.axis_index("col")
    tile = front[0]
    local_rows, block_size, local_cols = (tile.shape[0], tile.shape[1], tile.shape[2])
    matrix = tile.reshape(local_rows * block_size, local_cols * block_size)
    update = child_update[0]
    slab_rows, slab_cols = update.shape
    per_row = slab_rows // rows_count
    per_col = slab_cols // cols_count
    targets = child_map[0]
    target_block = targets // block_size
    target_within = targets % block_size
    target_row = target_block // rows_count * block_size + target_within
    target_col = target_block // cols_count * block_size + target_within
    row_order = jnp.argsort(
        (target_block % rows_count).reshape(rows_count, slab_rows), axis=1, stable=True
    )
    row_order = (
        row_order + (jnp.arange(rows_count, dtype=jnp.int32) * slab_rows)[:, None]
    ).reshape(rows_count, rows_count, per_row)
    col_order = jnp.argsort(
        (target_block % cols_count).reshape(cols_count, slab_cols), axis=1, stable=True
    )
    col_order = (
        col_order + (jnp.arange(cols_count, dtype=jnp.int32) * slab_cols)[:, None]
    ).reshape(cols_count, cols_count, per_col)
    send_rows = (jnp.take(row_order, row_place, axis=0) - row_place * slab_rows).reshape(-1)
    send_cols = (jnp.take(col_order, col_place, axis=0) - col_place * slab_cols).reshape(-1)
    recv_rows = target_row[jnp.take(row_order, row_place, axis=1).reshape(-1)]
    recv_cols = target_col[jnp.take(col_order, col_place, axis=1).reshape(-1)]
    outgoing = update[send_rows][:, send_cols].reshape(rows_count, per_row, cols_count, per_col)
    outgoing = outgoing.transpose(0, 2, 1, 3).reshape(rows_count * cols_count, per_row * per_col)
    landed = lax.all_to_all(outgoing, ("row", "col"), split_axis=0, concat_axis=0, tiled=True)
    landed = landed.reshape(rows_count, cols_count, per_row, per_col).transpose(0, 2, 1, 3)
    landed = landed.reshape(rows_count * per_row, cols_count * per_col)
    row_places = jnp.arange(local_rows * block_size, dtype=jnp.int32)
    col_places = jnp.arange(local_cols * block_size, dtype=jnp.int32)
    row_hits = (row_places[:, None] == recv_rows[None, :]).astype(jnp.float32)
    col_hits = (recv_cols[:, None] == col_places[None, :]).astype(jnp.float32)
    placed_rows = jnp.dot(row_hits, landed, precision=lax.Precision.HIGHEST)
    matrix = matrix + jnp.dot(placed_rows, col_hits, precision=lax.Precision.HIGHEST)
    leading = matrix[:, :block_size]
    panel_parts = []
    for root_col in range(PB):
        panel_parts.append(broadcast(leading, "col", root_col))
    panel_raw = jnp.concatenate(panel_parts, axis=1)
    upper_rows = panel_raw[:block_size]
    corner = lax.all_gather(upper_rows, "row", axis=0, tiled=True)[:PW]
    factor = jnp.linalg.cholesky(0.5 * (corner + corner.T))
    identity = jnp.eye(PW, dtype=jnp.float32)
    inverse = jax.scipy.linalg.solve_triangular(factor, identity, lower=True)
    solved = jnp.dot(panel_raw, inverse.T, precision=lax.Precision.HIGHEST)
    selected = (
        jnp.arange(local_cols, dtype=jnp.int32) * (cols_count // rows_count)
        + col_place // rows_count
    )
    candidate = solved.reshape(local_rows, block_size, PW)[selected].reshape(
        local_cols * block_size, PW
    )
    column_factor = broadcast(candidate, "row", col_place % rows_count)
    schur = jnp.dot(solved, column_factor.T, precision=lax.Precision.HIGHEST)
    block_rows = jnp.arange(local_rows, dtype=jnp.int32) * rows_count + row_place
    block_cols = jnp.arange(local_cols, dtype=jnp.int32) * cols_count + col_place
    pattern_here = pattern[0][block_rows[:, None], block_cols[None, :]]
    applied = (
        (pattern_here == 1) & (block_rows[:, None] >= PB) & (block_cols[None, :] >= PB)
    ).astype(jnp.float32)
    result = (
        matrix.reshape(local_rows, block_size, local_cols, block_size)
        - schur.reshape(local_rows, block_size, local_cols, block_size) * applied[:, None, :, None]
    )
    result = result.reshape(local_rows * block_size, local_cols * block_size)
    own_panel = lax.dynamic_slice_in_dim(
        solved, jnp.minimum(col_place, PB - 1) * block_size, block_size, 1
    )
    leading_new = jnp.where(col_place < PB, own_panel, result[:, :block_size])
    result = result.at[:, :block_size].set(leading_new)
    return result.reshape(1, local_rows, block_size, local_cols, block_size)


def solution(mesh):
    placed = (
        P("front", None, "row", None, "col"),
        P("front", "row", "col"),
        P("front", None),
        P("front", None, None),
    )
    return jax.shard_map(
        per_device,
        mesh=mesh,
        in_specs=placed,
        out_specs=P("front", None, "row", None, "col"),
        check_vma=False,
    )
```

profile of v0, /device:TPU:6, one launch (start us, length us, event | category | flops | bytes accessed | tf_op | source)
XLA Modules:
  0.0 1605.7 jit_solution(17670030128077399861)
XLA Ops:
  9.7 2.9 sort.21.cloned.1.call-done
  18.7 6.4 all-to-all-start
  25.4 44.2 %copy.42 = f32[1,12,256,12,256]{2,1,4,3,0:T(8,128)} copy(f32[1,12,256,12,256]{4,2,3,1,0:T(8,128)} %param.10) | data formatting | bytes 75497472 | tf_op jit(solution)/shard_map/reshape;squeeze | solution.py:22
  69.6 43.6 %copy.47 = f32[384,8,12,256]{3,1,2,0:T(8,128)} copy(f32[384,8,12,256]{3,2,1,0:T(8,128)} %bitcast.167) | data formatting | bytes 75497472
  113.3 3.1 gather_fusion
  116.5 3.1 gather_fusion.3
  120.3 5.4 fusion
  125.7 38.3 %convolution_add_fusion = f32[3072,3072]{0,1:T(8,128)} fusion(f32[3072,3072]{0,1:T(8,128)} %bitcast.168, f32[3072,512]{1,0:T(8,128)S(1)} %fusion, s32[512]{0:T(512)S(1)} %gather_fusion.3), kind=kOutput, calls=%fused_computation.9 | convolution fusion | flops 57993068544 | bytes 81790976 | tf_op jit(solution)/shard_map/dot_general | solution.py:58
  164.0 7.1 slice_select_fusion
  171.2 222.0 %all-reduce.7.cloned.1.call-done = (f32[3072,256]{0,1:T(8,128)}, f32[3072,256]{0,1:T(8,128)}, f32[3072,256]{0,1:T(8,128)}, f32[3072,256]{0,1:T(8,128)}) async-done(((f32[3072,256]{0,1:T(8,128)}, f32[3072,256]{0,1:T(8,128)}, f32[3072,256]{0,1:T(8,128)}, f32[3072,256]{0,1:T(8,128)}), (f32[3072,256]{0,1:T(8,128)}, f32[3072,256]{0,1:T(8,128)}, f32[3072,256]{0,1:T(8,128)}, ...) | async-done | bytes 12582928 | tf_op jit(solution)/shard_map/psum | solution.py:12
  393.2 2.3 constant_dynamic-update-slice_fusion.3
  398.8 4.6 copy-done.9
  404.9 2.5 fusion.26
  407.4 78.9 %all-gather.2.cloned.1.call-done = f32[1024,1024]{0,1:T(8,128)} async-done(((f32[256,1024]{0,1:T(8,128)}), f32[1024,1024]{0,1:T(8,128)}) %all-gather.2.cloned.1.call-update) | async-done | bytes 4194320 | tf_op jit(solution)/shard_map/all_gather | solution.py:65
  486.3 5.3 copy.33
  491.6 6.9 fusion.2
  498.5 5.5 copy.34
  504.0 4.4 fusion.1
  510.4 11.7 cholesky.223
  522.1 2.5 cholesky.255
  524.6 9.8 custom-call.63
  534.4 2.4 constant_dynamic-update-slice_fusion.29
  538.4 11.9 cholesky.244
  550.9 9.8 custom-call.64
  564.1 11.7 cholesky.468
  576.4 9.8 custom-call.65
  587.4 2.3 convolution_subtract_fusion.7
  589.8 12.1 cholesky.487
  602.5 9.8 custom-call.66
  613.4 2.4 convolution_subtract_fusion.8
  615.8 11.7 cholesky.506
  628.2 10.0 custom-call.67
  639.2 2.3 convolution_subtract_fusion.9
  641.5 11.7 cholesky.526
  653.8 9.8 custom-call.68
  666.6 11.7 cholesky.546
  679.0 9.8 custom-call.69
  691.4 11.7 cholesky.564
  714.1 4.8 select_select_fusion.1
  718.8 22.9 %while.4 = (s32[]{:T(128)}, f32[1024,1024]{1,0:T(8,128)}, s32[8,2]{0,1:T(2,128)S(1)}, f32[8,128,128]{2,1,0:T(8,128)S(1)}, s32[]{:T(128)}) while((s32[]{:T(128)}, f32[1024,1024]{1,0:T(8,128)}, s32[8,2]{0,1:T(2,128)S(1)}, f32[8,128,128]{2,1,0:T(8,128)S(1)}, s32[]{:T(128)}) %tuple.80), condition=%wide.while_cond.3, body=%wide.while_body.3.sunk | while | flops 2 | bytes 131189 | solution.py:68
  719.5 2.2 bitcast_dynamic-update-slice_fusion.2
  722.3 2.2 bitcast_dynamic-update-slice_fusion.2
  725.2 2.2 bitcast_dynamic-update-slice_fusion.2
  728.1 2.2 bitcast_dynamic-update-slice_fusion.2
  733.8 2.2 bitcast_dynamic-update-slice_fusion.2
  736.7 2.2 bitcast_dynamic-update-slice_fusion.2
  741.7 79.1 %custom-call.70 = f32[8,128,128]{1,2,0:T(8,128)S(1)} custom-call(f32[8,128,128]{2,1,0:T(8,128)S(1)} %get-tuple-element.44), custom_call_target="InvertDiagBlocksLowerTriangular" | custom-call | tf_op jit(solution)/shard_map/jit(_solve_triangular)/triangular_solve | solution.py:68
  829.2 2.4 fusion.23
  832.3 2.8 convolution_subtract_fusion.2
  835.8 3.0 convolution_subtract_fusion.1
  839.5 3.3 convolution_subtract_fusion.3
  843.4 82.1 %fusion.98 = f32[3072,1024]{1,0:T(8,128)} fusion(f32[3072,1024]{0,1:T(8,128)S(1)} %bitcast.175, f32[1024,1024]{1,0:T(8,128)S(1)} %convolution_dynamic-update-slice_fusion), kind=kOutput, calls=%fused_computation.250 | convolution fusion | flops 38654705664 | bytes 29360128 | tf_op jit(solution)/shard_map/dot_general | solution.py:69
  925.5 11.5 gather_fusion.4
  937.0 7.5 broadcast_select_fusion
  947.7 17.1 %mul.65 = f32[12,256,12,256]{3,2,1,0:T(8,128)} broadcast(f32[12,12]{1,0:T(8,128)S(1)} %and_convert_fusion), dimensions={0,2} | broadcast | bytes 37749312 | tf_op jit(solution)/shard_map/mul | solution.py:87
  964.7 43.7 %copy.49 = f32[384,8,12,256]{3,1,2,0:T(8,128)} copy(f32[384,8,12,256]{3,2,1,0:T(8,128)} %bitcast.166) | data formatting | bytes 75497472
  1008.4 37.1 %copy.36 = f32[3072,3072]{0,1:T(8,128)} copy(f32[3072,3072]{1,0:T(8,128)} %bitcast.169) | data formatting | bytes 75497472 | tf_op jit(solution)/shard_map/mul | solution.py:87
  1046.1 3.8 constant_dynamic-slice_fusion.1
  1049.9 3.8 copy.46
  1053.7 320.1 %all-reduce.5.cloned.1.call-done = f32[3072,1024]{1,0:T(8,128)} async-done(((f32[3072,1024]{1,0:T(8,128)}), f32[3072,1024]{1,0:T(8,128)}) %all-reduce.5.cloned.1.call-update) | async-done | bytes 12582928 | tf_op jit(solution)/shard_map/psum | solution.py:12
  1373.9 129.6 %multiply_subtract_fusion = f32[3072,3072]{0,1:T(8,128)} fusion(f32[3072,3072]{0,1:T(8,128)} %convolution_add_fusion, f32[3072,3072]{0,1:T(8,128)} %copy.36, f32[3072,1024]{1,0:T(8,128)} %fusion.98, f32[3072,1024]{1,0:T(8,128)} %all-reduce.5.cloned.1.call-done), kind=kOutput, calls=%fused_computation.8 | convolution fusion | flops 115982991360 | bytes 138412032 | tf_op jit(solution)/shard_map/dot_general | solution.py:78
  1503.5 4.6 fusion.3
  1508.2 45.2 %reshape.534 = f32[1,12,256,12,256]{2,1,4,3,0:T(8,128)} reshape(f32[3072,3072]{0,1:T(8,128)} %fusion.3) | data formatting | bytes 75497472 | tf_op jit(solution)/shard_map/reshape | solution.py:95
  1553.4 45.6 %copy.39 = f32[1,12,256,12,256]{4,2,3,1,0:T(8,128)} copy(f32[1,12,256,12,256]{2,1,4,3,0:T(8,128)} %reshape.534) | data formatting | bytes 75497472 | tf_op jit(solution)/shard_map/reshape | solution.py:95
  (140 shorter events, 65.0 us)
Async XLA Ops:
  6.5 6.9 copy-start
  6.5 6.0 sort.21.cloned.1.call-start
  18.7 100.9 %all-to-all-start = ((f32[16,1,16384]{2,1,0:T(1,128)}), f32[16,1,16384]{2,1,0:T(1,128)S(1)}, u32[]{:S(2)}, u32[]{:S(2)}) async-start(f32[16,1,16384]{2,1,0:T(1,128)} %bitcast.14), calls=%async_computation | async-start | bytes 2097152 | tf_op jit(solution)/shard_map/all_to_all | solution.py:50
  25.1 368.1 %all-reduce.7.cloned.1.call-start = ((), (), s32[]{:S(2)}) async-start(), calls=%async_computation.3 | async-start | bytes 25165824 | tf_op jit(solution)/shard_map/psum | solution.py:12
  69.6 43.6 %copy-start.10 = (s32[1,2048]{1,0:T(1,128)S(1)}, s32[1,2048]{1,0:T(1,128)}, u32[]{:S(2)}) copy-start(s32[1,2048]{1,0:T(1,128)} %param.12) | copy-start | bytes 24580
  171.1 315.2 %all-gather.2.cloned.1.call-start = ((), (), s32[]{:S(2)}) async-start(), calls=%async_computation.1 | async-start | bytes 5242880 | tf_op jit(solution)/shard_map/all_gather | solution.py:65
  393.2 2.8 copy-start.8
  395.4 2.0 copy-start.7
  396.3 2.1 copy-start.6
  398.8 4.6 copy-start.9
  404.5 969.4 %all-reduce.5.cloned.1.call-start = ((), (), s32[]{:S(2)}) async-start(), calls=%async_computation.2 | async-start | bytes 25165824 | tf_op jit(solution)/shard_map/psum | solution.py:12
  508.4 1.9 copy-start.5
  820.8 3.2 copy-start.3
  829.2 14.2 slice-start
  832.3 11.1 slice-start.1
  835.8 7.6 slice-start.2
  944.5 0.7 copy-start.2
  1373.9 129.7 %copy-start.4 = (f32[3072,256]{0,1:T(8,128)S(1)}, f32[3072,256]{0,1:T(8,128)}, u32[]{:S(2)}) copy-start(f32[3072,256]{0,1:T(8,128)} %copy.46) | copy-start | bytes 9437188
  1553.4 45.6 %copy-start.1 = (f32[1,512,512]{2,1,0:T(8,128)S(1)}, f32[1,512,512]{2,1,0:T(8,128)}, u32[]{:S(2)}) copy-start(f32[1,512,512]{2,1,0:T(8,128)} %param.11) | copy-start | bytes 3145732
Sparse Core Ops, SparseCore 0:
  9.8 2.4 sort.23.cloned.1.call-done
  171.3 221.8 all-reduce.6
  404.6 81.6 all-gather.1
  944.6 429.1 all-reduce.4
  (1 shorter events, 0.0 us)
where the time goes:
time: 1610 us
  waiting for transfers between devices  621 us (39%)
  local copies, waits for them, and re-layouts  364 us (23%)
  matrix products  301 us (19%)
  other arithmetic  294 us (18%)
  between operations  19 us (1%)
    psum x2, waiting for transfers between devices, broadcast(): return lax.psum(kept, axis)  542 us
    another operation x31, other arithmetic, per_device(): factor = jnp.linalg.cholesky(0.5 * (corner + corner.T))  173 us
    dot_general x1, matrix products, per_device(): schur = jnp.dot(solved, column_factor.T, precision=lax.Precision.HIGHEST)  130 us
    unnamed x36, local copies, waits for them, and re-layouts  104 us
    reshape x2, local copies, waits for them, and re-layouts, per_device(): return result.reshape(1, local_rows, block_size, local_cols, block_size)  90.8 us
    another operation x3, other arithmetic, per_device(): inverse = jax.scipy.linalg.solve_triangular(factor, identity, lower=True)  83.9 us
    dot_general x1, matrix products, per_device(): solved = jnp.dot(panel_raw, inverse.T, precision=lax.Precision.HIGHEST)  82.1 us
    all_gather x1, waiting for transfers between devices, per_device(): corner = lax.all_gather(upper_rows, 'row', axis=0, tiled=True)[:PW]  78.9 us
  transfers between devices with their start and end apart: 4, of which 3 were waited for; matrix products, arithmetic and copies ran while one was open for 13% of the time, Pallas kernels for 0%

commit v1 on v0

v1 whole, which is shorter than its diff:
```python
import functools

import jax
import jax.numpy as jnp
from jax import lax
from jax.experimental import pallas as pl
from jax.experimental.pallas import tpu as pltpu
from jax.sharding import PartitionSpec as P

PB = 4
PW = 1024
DB = 128


def broadcast(value, axis, source):
    kept = jnp.where(lax.axis_index(axis) == source, value, 0).astype(value.dtype)
    return lax.psum(kept, axis)


def exact_dot(left, right):
    return jnp.dot(left, right, precision=lax.Precision.HIGHEST, preferred_element_type=jnp.float32)


def factor_inverse_kernel(corner_ref, high_ref, low_ref, inv_ref, work_ref, diag_ref, unit_ref):
    work_ref[...] = corner_ref[...]
    inv_ref[...] = jnp.zeros_like(inv_ref)
    lanes = lax.broadcasted_iota(jnp.int32, (DB, DB), 1)
    rows = lax.broadcasted_iota(jnp.int32, (DB, DB), 0)
    quarter = DB // 4
    for start in range(0, PW, DB):
        stop = start + DB
        diag_ref[...] = work_ref[start:stop, start:stop]
        unit_ref[...] = (lanes == rows).astype(jnp.float32)
        for first in range(0, DB, quarter):
            lane_ids = lanes[first:]
            row_ids = rows[first:]

            def eliminate(place, carry):
                pivot_row = diag_ref[pl.ds(place, 1), :]
                unit_row = unit_ref[pl.ds(place, 1), :]
                lower = diag_ref[first:, :]
                pivot = jnp.sum(jnp.where(lanes[:1] == place, pivot_row, 0.0), axis=1, keepdims=True)
                column = jnp.sum(jnp.where(lane_ids == place, lower, 0.0), axis=1, keepdims=True)
                scale = jnp.where(row_ids > place, column * (1.0 / pivot), 0.0)
                diag_ref[first:, :] = lower - scale * pivot_row
                unit_ref[first:, :] = unit_ref[first:, :] - scale * unit_row
                return carry

            lax.fori_loop(first, first + quarter, eliminate, 0)
        pivots = jnp.sum(jnp.where(lanes == rows, diag_ref[...], 0.0), axis=1, keepdims=True)
        block_inverse = unit_ref[...] / jnp.sqrt(pivots)
        inv_ref[start:stop, start:stop] = block_inverse
        if start:
            inv_ref[start:stop, :start] = exact_dot(block_inverse, inv_ref[start:stop, :start])
        if stop < PW:
            upper = exact_dot(block_inverse, work_ref[start:stop, stop:])
            below = upper.T
            work_ref[stop:, stop:] = work_ref[stop:, stop:] - exact_dot(below, upper)
            inv_ref[stop:, :stop] = inv_ref[stop:, :stop] - exact_dot(below, inv_ref[start:stop, :stop])
    high_ref[...], low_ref[...] = split_two(inv_ref[...])


def factor_inverse(corner):
    return pl.pallas_call(
        factor_inverse_kernel,
        out_shape=[jax.ShapeDtypeStruct((PW, PW), jnp.bfloat16)] * 2,
        in_specs=[pl.BlockSpec(memory_space=pltpu.VMEM)],
        out_specs=[pl.BlockSpec(memory_space=pltpu.VMEM)] * 2,
        scratch_shapes=[
            pltpu.VMEM((PW, PW), jnp.float32),
            pltpu.VMEM((PW, PW), jnp.float32),
            pltpu.VMEM((DB, DB), jnp.float32),
            pltpu.VMEM((DB, DB), jnp.float32),
        ],
        compiler_params=pltpu.CompilerParams(vmem_limit_bytes=48 * 1024 * 1024),
        cost_estimate=pl.CostEstimate(flops=100_000_000_000, bytes_accessed=8 * PW * PW, transcendentals=0),
        name="factor_inverse",
    )(corner)


def split_two(value):
    high = value.astype(jnp.bfloat16)
    low = (value - high.astype(jnp.float32)).astype(jnp.bfloat16)
    return high, low


def matmul(left, right):
    return jnp.dot(left, right, preferred_element_type=jnp.float32)


def matmul_nt(left, right):
    return lax.dot_general(left, right, (((1,), (1,)), ((), ())), preferred_element_type=jnp.float32)


def place_kernel(front_ref, rows_ref, hits_ref, out_ref):
    values = rows_ref[...]
    high = values.astype(jnp.bfloat16)
    rest = values - high.astype(jnp.float32)
    middle, low = split_two(rest)
    block_size = out_ref.shape[-1]
    for m in range(out_ref.shape[2]):
        hits = hits_ref[:, m * block_size:(m + 1) * block_size]
        added = matmul(low, hits) + matmul(middle, hits) + matmul(high, hits)
        out_ref[0, 0, m] = front_ref[0, 0, m] + added


def place_children(front, placed_rows, col_hits):
    _, local_rows, local_cols, block_size, _ = front.shape
    count = placed_rows.shape[1]
    spec = pl.BlockSpec((1, 1, local_cols, block_size, block_size), lambda i: (0, i, 0, 0, 0))
    return pl.pallas_call(
        place_kernel,
        grid=(local_rows,),
        out_shape=jax.ShapeDtypeStruct(front.shape, jnp.float32),
        in_specs=[
            spec,
            pl.BlockSpec((block_size, count), lambda i: (i, 0)),
            pl.BlockSpec(col_hits.shape, lambda i: (0, 0)),
        ],
        out_specs=spec,
        compiler_params=pltpu.CompilerParams(vmem_limit_bytes=40 * 1024 * 1024),
        cost_estimate=pl.CostEstimate(
            flops=6 * front.size * count, bytes_accessed=8 * front.size, transcendentals=0
        ),
        name="place_children",
    )(front, placed_rows, col_hits)


def solve_kernel(split, raw_ref, high_ref, low_ref, *out_refs):
    block_size = raw_ref.shape[-1]
    pieces = [split_two(raw_ref[k]) for k in range(PB)]
    for n in range(PB):
        total = None
        for k in range(n + 1):
            raw_high, raw_low = pieces[k]
            here = (slice(n * block_size, (n + 1) * block_size), slice(k * block_size, (k + 1) * block_size))
            inv_high, inv_low = high_ref[here], low_ref[here]
            term = matmul_nt(raw_low, inv_high) + matmul_nt(raw_high, inv_low) + matmul_nt(raw_high, inv_high)
            total = term if total is None else total + term
        columns = slice(n * block_size, (n + 1) * block_size)
        if split:
            out_refs[0][:, columns], out_refs[1][:, columns] = split_two(total)
        else:
            out_refs[0][:, columns] = total


def solve_rows(raw, inv_high, inv_low, split):
    parts, rows, block_size = raw.shape
    out_spec = pl.BlockSpec((block_size, PW), lambda i: (i, 0))
    if split:
        out_shape = [jax.ShapeDtypeStruct((rows, PW), jnp.bfloat16)] * 2
    else:
        out_shape = [jax.ShapeDtypeStruct((rows, PW), jnp.float32)]
    whole = pl.BlockSpec((PW, PW), lambda i: (0, 0))
    return pl.pallas_call(
        functools.partial(solve_kernel, split),
        grid=(rows // block_size,),
        out_shape=out_shape,
        in_specs=[pl.BlockSpec((parts, block_size, block_size), lambda i: (0, i, 0)), whole, whole],
        out_specs=[out_spec] * len(out_shape),
        compiler_params=pltpu.CompilerParams(vmem_limit_bytes=40 * 1024 * 1024),
        cost_estimate=pl.CostEstimate(
            flops=4 * rows * PW * PW, bytes_accessed=8 * rows * PW, transcendentals=0
        ),
        name="solve_rows",
    )(raw, inv_high, inv_low)


def schur_kernel(kept_ref, own_ref, sum_ref, solved_ref, high_ref, low_ref, out_ref):
    i = pl.program_id(0)
    block_size = out_ref.shape[-1]
    solved_high, solved_low = split_two(solved_ref[...])
    for m in range(out_ref.shape[2]):
        rows = slice(m * block_size, (m + 1) * block_size)
        kept = kept_ref[i, m] == 1

        @pl.when(kept)
        def _():
            high, low = high_ref[rows, :], low_ref[rows, :]
            product = matmul_nt(solved_low, high) + matmul_nt(solved_high, low) + matmul_nt(solved_high, high)
            out_ref[0, 0, m] = sum_ref[0, 0, m] - product

        @pl.when(jnp.logical_not(kept))
        def _():
            out_ref[0, 0, m] = sum_ref[0, 0, m]

    @pl.when(own_ref[0] < PB)
    def _():
        place = pl.multiple_of(jnp.minimum(own_ref[0], PB - 1) * block_size, block_size)
        out_ref[0, 0, 0] = solved_ref[:, pl.ds(place, block_size)]


def schur_update(kept, own, summed, solved, col_high, col_low):
    _, local_rows, local_cols, block_size, _ = summed.shape
    spec = pl.BlockSpec((1, 1, local_cols, block_size, block_size), lambda i, *_: (0, i, 0, 0, 0))
    whole = pl.BlockSpec(
        col_high.shape, lambda i, *_: (0, 0), pipeline_mode=pl.Buffered(buffer_count=1)
    )
    return pl.pallas_call(
        schur_kernel,
        out_shape=jax.ShapeDtypeStruct(summed.shape, jnp.float32),
        grid_spec=pltpu.PrefetchScalarGridSpec(
            num_scalar_prefetch=2,
            grid=(local_rows,),
            in_specs=[spec, pl.BlockSpec((block_size, PW), lambda i, *_: (i, 0)), whole, whole],
            out_specs=spec,
        ),
        input_output_aliases={2: 0},
        compiler_params=pltpu.CompilerParams(vmem_limit_bytes=52 * 1024 * 1024),
        cost_estimate=pl.CostEstimate(
            flops=6 * summed.size * PW, bytes_accessed=8 * summed.size, transcendentals=0
        ),
        name="schur_update",
    )(kept, own, summed, solved, col_high, col_low)


def per_device(front, child_update, child_map, pattern):
    rows_count = lax.axis_size("row")
    cols_count = lax.axis_size("col")
    row_place = lax.axis_index("row")
    col_place = lax.axis_index("col")
    blocks = front.transpose(0, 1, 3, 2, 4)
    local_rows, local_cols, block_size = blocks.shape[1:4]
    update = child_update[0]
    slab_rows, slab_cols = update.shape
    per_row = slab_rows // rows_count
    per_col = slab_cols // cols_count
    targets = child_map[0]
    target_block = targets // block_size
    target_within = targets % block_size
    target_row = target_block // rows_count * block_size + target_within
    target_col = target_block // cols_count * block_size + target_within
    row_order = jnp.argsort(
        (target_block % rows_count).reshape(rows_count, slab_rows), axis=1, stable=True
    )
    row_order = (
        row_order + (jnp.arange(rows_count, dtype=jnp.int32) * slab_rows)[:, None]
    ).reshape(rows_count, rows_count, per_row)
    col_order = jnp.argsort(
        (target_block % cols_count).reshape(cols_count, slab_cols), axis=1, stable=True
    )
    col_order = (
        col_order + (jnp.arange(cols_count, dtype=jnp.int32) * slab_cols)[:, None]
    ).reshape(cols_count, cols_count, per_col)
    send_rows = (jnp.take(row_order, row_place, axis=0) - row_place * slab_rows).reshape(-1)
    send_cols = (jnp.take(col_order, col_place, axis=0) - col_place * slab_cols).reshape(-1)
    recv_rows = target_row[jnp.take(row_order, row_place, axis=1).reshape(-1)]
    recv_cols = target_col[jnp.take(col_order, col_place, axis=1).reshape(-1)]
    outgoing = update[send_rows][:, send_cols].reshape(rows_count, per_row, cols_count, per_col)
    outgoing = outgoing.transpose(0, 2, 1, 3).reshape(rows_count * cols_count, per_row * per_col)
    landed = lax.all_to_all(outgoing, ("row", "col"), split_axis=0, concat_axis=0, tiled=True)
    landed = landed.reshape(rows_count, cols_count, per_row, per_col).transpose(0, 2, 1, 3)
    landed = landed.reshape(rows_count * per_row, cols_count * per_col)
    row_places = jnp.arange(local_rows * block_size, dtype=jnp.int32)
    col_places = jnp.arange(local_cols * block_size, dtype=jnp.int32)
    row_hits = (row_places[:, None] == recv_rows[None, :]).astype(jnp.float32)
    col_hits = (recv_cols[:, None] == col_places[None, :]).astype(jnp.float32)
    placed_rows = jnp.dot(row_hits, landed, precision=lax.Precision.HIGHEST)
    leading = blocks[0, :, 0].reshape(local_rows * block_size, block_size)
    leading = leading + jnp.dot(
        placed_rows, col_hits[:, :block_size], precision=lax.Precision.HIGHEST
    )
    square = rows_count == cols_count == PB
    if square:
        corner = lax.all_gather(leading[:block_size], "row", axis=0, tiled=True)
        corner = lax.all_gather(corner, "col", axis=1, tiled=True)
        corner, leading = lax.optimization_barrier((corner, leading))
        panel_raw = lax.all_gather(leading, "col", axis=0, tiled=False)
        swap = [
            (p * cols_count + q, q * cols_count + p)
            for p in range(rows_count)
            for q in range(cols_count)
        ]
        swapped = lax.ppermute(leading, ("row", "col"), swap)
        column_raw = lax.all_gather(swapped, "row", axis=0, tiled=False)
    else:
        panel_parts = []
        for root_col in range(PB):
            panel_parts.append(broadcast(leading, "col", root_col))
        panel_raw = jnp.stack(panel_parts)
        upper_rows = jnp.concatenate([part[:block_size] for part in panel_parts], axis=1)
        corner = lax.all_gather(upper_rows, "row", axis=0, tiled=True)[:PW]
        selected = (
            jnp.arange(local_cols, dtype=jnp.int32) * (cols_count // rows_count)
            + col_place // rows_count
        )
        candidate = panel_raw.reshape(PB, local_rows, block_size, block_size)[:, selected]
        candidate = candidate.reshape(PB, local_cols * block_size, block_size)
        column_raw = broadcast(candidate, "row", col_place % rows_count)
    summed = place_children(blocks, placed_rows, col_hits.astype(jnp.bfloat16))
    inv_high, inv_low = factor_inverse(0.5 * (corner + corner.T))
    (solved,) = solve_rows(panel_raw, inv_high, inv_low, False)
    col_high, col_low = solve_rows(column_raw, inv_high, inv_low, True)
    block_rows = jnp.arange(local_rows, dtype=jnp.int32) * rows_count + row_place
    block_cols = jnp.arange(local_cols, dtype=jnp.int32) * cols_count + col_place
    pattern_here = pattern[0][block_rows[:, None], block_cols[None, :]]
    applied = (
        (pattern_here == 1) & (block_rows[:, None] >= PB) & (block_cols[None, :] >= PB)
    ).astype(jnp.int32)
    own = jnp.full((1,), col_place, jnp.int32)
    result = schur_update(applied, own, summed, solved, col_high, col_low)
    return result.transpose(0, 1, 3, 2, 4)


def solution(mesh):
    placed = (
        P("front", None, "row", None, "col"),
        P("front", "row", "col"),
        P("front", None),
        P("front", None, None),
    )
    return jax.shard_map(
        per_device,
        mesh=mesh,
        in_specs=placed,
        out_specs=P("front", None, "row", None, "col"),
        check_vma=False,
    )
```

time: 1610 us -> 606 us (0.38)
  waiting for transfers between devices: 621 us -> 222 us
  local copies, waits for them, and re-layouts: 364 us -> 70 us
  matrix products: 301 us -> 11.6 us
  other arithmetic: 294 us -> 12.9 us
  Pallas kernels: 0 us -> 255 us
    psum x2 -> x0, waiting for transfers between devices: 542 us -> none  [broadcast(): return lax.psum(kept, axis)]
    another operation x35 -> x0, other arithmetic: 257 us -> none  [the longest x31 173 us: per_device(): factor = jnp.linalg.cholesky(0.5 * (corner + corner.T))]
    pallas_call x0 -> x5, Pallas kernels: none -> 255 us  [the longest x1 123 us: factor_inverse(): pl.pallas_call(factor_inverse_kernel, out_shape=[jax.ShapeDtypeStruct((PW...]
    dot_general x3 -> x1, matrix products: 250 us -> 6.01 us  [per_device(): jnp.dot(placed_rows, col_hits[:, :block_size], precision=lax.Precision.HI...]
    ppermute x0 -> x1, waiting for transfers between devices: none -> 137 us  [per_device(): swapped = lax.ppermute(leading, ('row', 'col'), swap)]
    reshape x2 -> x0, local copies, waits for them, and re-layouts: 90.8 us -> none  [per_device(): return result.reshape(1, local_rows, block_size, local_cols, block_size)]
    unnamed x36 -> x24, local copies, waits for them, and re-layouts: 104 us -> 13.3 us
    another operation x34 -> x1, local copies, waits for them, and re-layouts: 69.5 us -> 2.36 us  [per_device(): leading = blocks[0, :, 0].reshape(local_rows * block_size, block_size)]
  transfers between devices with their start and end apart: 4 -> 6, of which waited for: 3 -> 5; matrix products, arithmetic and copies ran while one was open for 13% -> 7% of each run, Pallas kernels for 0% -> 30%
where the time goes in v1:
time: 606 us; the launch traced here: 597 us
  Pallas kernels  255 us (42%)
  waiting for transfers between devices  222 us (37%)
  local copies, waits for them, and re-layouts  70 us (12%)
  between operations  13.6 us (2%)
  other arithmetic  12.9 us (2%)
  starting transfers between devices  11.7 us (2%)
  matrix products  11.6 us (2%)
    ppermute x1, waiting for transfers between devices, per_device(): swapped = lax.ppermute(leading, ('row', 'col'), swap)  137 us
    pallas_call x1, Pallas kernels, factor_inverse(): pl.pallas_call(factor_inverse_kernel, out_shape=[jax.ShapeDtypeStruct((PW...  123 us
    pallas_call x1, Pallas kernels, schur_update(): pl.pallas_call(schur_kernel, out_shape=jax.ShapeDtypeStruct(summed.shape,...  57.1 us
    pallas_call x1, Pallas kernels, place_children(): pl.pallas_call(place_kernel, grid=(local_rows,), out_shape=jax.ShapeDtype...  38.1 us
    pallas_call x2, Pallas kernels, solve_rows(): pl.pallas_call(functools.partial(solve_kernel, split), grid=(rows // bloc...  37.4 us
    all_gather x1, waiting for transfers between devices, per_device(): corner = lax.all_gather(corner, 'col', axis=1, tiled=True)  34.6 us
    all_gather x1, waiting for transfers between devices, per_device(): corner = lax.all_gather(leading[:block_size], 'row', axis=0, tiled=True)  29.9 us
    unnamed x24, local copies, waits for them, and re-layouts  13.3 us
  transfers between devices with their start and end apart: 6, of which 5 were waited for; matrix products, arithmetic and copies ran while one was open for 7% of the time, Pallas kernels for 30%

profile of v1, /device:TPU:6, one launch (start us, length us, event | category | flops | bytes accessed | tf_op | source)
XLA Modules:
  0.0 597.1 jit_solution(6214745345810260790)
XLA Ops:
  6.5 0.0 copy-start
  6.5 0.0 sort.21.cloned.1.call-start
  6.5 0.5 broadcast.346
  7.1 1.4 reduce.3
  8.4 0.6 add_select_fusion
  9.1 0.6 iota.36
  9.6 0.0 sort.21.cloned.1.call-update
  9.7 2.8 sort.21.cloned.1.call-done
  12.5 0.8 broadcast_add_fusion
  13.4 0.0 copy-done
  13.4 1.6 gather_fusion.2
  15.0 0.3 copy.20
  15.4 1.6 gather_fusion.3
  17.0 0.4 reshape.190
  17.4 1.3 copy.21
  18.7 6.4 %all-to-all-start = ((f32[16,1,16384]{2,1,0:T(1,128)}), f32[16,1,16384]{2,1,0:T(1,128)}, u32[]{:S(2)}, u32[]{:S(2)}) async-start(f32[16,1,16384]{2,1,0:T(1,128)} %bitcast.17), calls=%async_computation | async-start | bytes 2097152 | tf_op jit(solution)/shard_map/all_to_all | solution.py:251
  25.1 0.0 all-gather.7.cloned.1.call-start
  25.1 2.3 slice.40
  27.4 0.0 copy-start.10
  27.4 2.4 copy.24
  29.8 0.0 copy-done.10
  29.8 3.1 gather_fusion.1
  33.0 3.3 gather_fusion.4
  36.3 3.0 iota_compare_fusion
  39.3 8.6 %all-to-all-done = f32[16,1,16384]{2,1,0:T(1,128)} async-done(((f32[16,1,16384]{2,1,0:T(1,128)}), f32[16,1,16384]{2,1,0:T(1,128)}, u32[]{:S(2)}, u32[]{:S(2)}) %all-to-all-start) | async-done | bytes 1048608 | tf_op jit(solution)/shard_map/all_to_all | solution.py:251
  48.0 1.9 copy.23
  49.9 0.0 copy-start.9
  49.9 5.6 fusion.rows_ref
  55.5 6.0 %convolution_add_fusion = f32[3072,256]{0,1:T(8,128)} fusion(f32[3072,256]{0,1:T(8,128)S(1)} %copy-done.9, f32[3072,512]{1,0:T(8,128)S(1)} %fusion.rows_ref, pred[512,3072]{1,0:T(32,128)(4,1)} %get-tuple-element.47), kind=kOutput, calls=%fused_computation.11 | convolution fusion | flops 4832624640 | bytes 12713984 | tf_op jit(solution)/shard_map/dot_general | solution.py:260
  61.5 2.7 copy-done.2
  64.2 1.7 slice.42
  65.9 0.0 all-gather.7.cloned.1.call-update
  65.9 0.0 all-gather.9.cloned.1.call-start
  66.0 29.9 %all-gather.7.cloned.1.call-done = f32[1024,256]{0,1:T(8,128)} async-done(((f32[256,256]{0,1:T(8,128)}), f32[1024,256]{0,1:T(8,128)}) %all-gather.7.cloned.1.call-update) | async-done | bytes 1048592 | tf_op jit(solution)/shard_map/all_gather | solution.py:265
  95.8 0.0 all-gather.9.cloned.1.call-update
  95.9 0.0 all-gather.11.cloned.1.call-start
  95.9 34.6 %all-gather.9.cloned.1.call-done = f32[1024,1024]{0,1:T(8,128)} async-done(((f32[1024,256]{0,1:T(8,128)}), f32[1024,1024]{0,1:T(8,128)}) %all-gather.9.cloned.1.call-update) | async-done | bytes 4194320 | tf_op jit(solution)/shard_map/all_gather | solution.py:266
  130.5 0.0 all-gather.11.cloned.1.call-update
  130.5 0.0 all-gather.13.cloned.1.call-start
  130.6 5.2 collective-permute-start
  135.8 136.7 %collective-permute-done = f32[3072,256]{0,1:T(8,128)} collective-permute-done((f32[3072,256]{0,1:T(8,128)}, f32[3072,256]{0,1:T(8,128)}, u32[]{:S(2)}, u32[]{:S(2)}) %collective-permute-start) | collective-permute-done | bytes 3145760 | tf_op jit(solution)/shard_map/ppermute | solution.py:274
  272.4 0.0 all-gather.13.cloned.1.call-update
  272.5 0.1 broadcast_or_fusion
  272.6 0.1 reshape.294
  272.6 0.0 copy-done.8
  272.7 2.4 gather_fusion
  275.1 0.1 reshape.335
  275.2 0.1 and_convert_fusion.kept_ref
  275.3 2.9 copy-done.3
  278.2 38.1 %place_children.1.sum_ref = f32[1,12,12,256,256]{4,3,2,1,0:T(8,128)} custom-call(f32[1,12,12,256,256]{4,3,2,1,0:T(8,128)} %bitcast.59, f32[3072,512]{1,0:T(8,128)S(1)} %copy-done.3, bf16[512,3072]{1,0:T(8,128)(2,1)S(1)} %get-tuple-element.48.hits_ref), custom_call_target="tpu_custom_call" | custom-call | flops 28991029248 | bytes 75497472 | tf_op jit(solution)/shard_map/place_children/pallas_call | solution.py:111
  316.3 5.4 copy.27
  321.7 6.9 %fusion.1.corner_ref = f32[1024,1024]{1,0:T(8,128)} fusion(f32[1024,1024]{1,0:T(8,128)} %copy.27, f32[1024,1024]{0,1:T(8,128)} %all-gather.9.cloned.1.call-done), kind=kLoop, calls=%fused_computation.10 | loop fusion | flops 2097152 | bytes 12582912 | tf_op jit(solution)/shard_map/mul | solution.py:291
  328.6 122.7 %factor_inverse.1 = (bf16[1024,1024]{1,0:T(8,128)(2,1)S(1)}, bf16[1024,1024]{1,0:T(8,128)(2,1)S(1)}) custom-call(f32[1024,1024]{1,0:T(8,128)} %fusion.1.corner_ref), custom_call_target="tpu_custom_call" | custom-call | flops 99999997952 | bytes 8388608 | tf_op jit(solution)/shard_map/factor_inverse/pallas_call | solution.py:64
  451.3 0.0 copy-start.5
  451.3 1.3 copy-done.5
  452.6 12.6 %copy.26 = f32[12288,256]{1,0:T(8,128)} copy(f32[12288,256]{0,1:T(8,128)} %all-gather.11.cloned.1.call-done) | data formatting | bytes 25165824 | tf_op jit(solution)/shard_map/all_gather | solution.py:268
  465.2 1.6 copy-done.6
  466.8 19.5 %solve_rows.2.solved_ref = f32[3072,1024]{1,0:T(8,128)} custom-call(f32[4,3072,256]{2,1,0:T(8,128)} %bitcast.54, bf16[1024,1024]{1,0:T(8,128)(2,1)S(1)} %get-tuple-element.17.high_ref, bf16[1024,1024]{1,0:T(8,128)(2,1)S(1)} %copy-done.6), custom_call_target="tpu_custom_call" | custom-call | flops 12884901888 | bytes 25165824 | tf_op jit(solution)/shard_map/solve_rows/pallas_call | solution.py:155
  486.3 12.2 %all-gather.13.cloned.1.call-done = f32[12288,256]{0,1:T(8,128)} async-done(((f32[3072,256]{0,1:T(8,128)}), f32[12288,256]{0,1:T(8,128)}) %all-gather.13.cloned.1.call-update) | async-done | bytes 12582928 | tf_op jit(solution)/shard_map/all_gather | solution.py:275
  498.5 12.6 %copy.28 = f32[12288,256]{1,0:T(8,128)} copy(f32[12288,256]{0,1:T(8,128)} %all-gather.13.cloned.1.call-done) | data formatting | bytes 25165824 | tf_op jit(solution)/shard_map/all_gather | solution.py:275
  511.1 1.6 copy-done.7
  512.7 18.0 %solve_rows.3 = (bf16[3072,1024]{1,0:T(8,128)(2,1)S(1)}, bf16[3072,1024]{1,0:T(8,128)(2,1)}) custom-call(f32[4,3072,256]{2,1,0:T(8,128)} %bitcast.53, bf16[1024,1024]{1,0:T(8,128)(2,1)S(1)} %get-tuple-element.17.high_ref, bf16[1024,1024]{1,0:T(8,128)(2,1)S(1)} %copy-done.7), custom_call_target="tpu_custom_call" | custom-call | flops 12884901888 | bytes 25165824 | tf_op jit(solution)/shard_map/solve_rows/pallas_call | solution.py:155
  530.7 2.6 copy-done.4
  533.3 57.1 %schur_update.1 = f32[1,12,12,256,256]{4,3,2,1,0:T(8,128)} custom-call(s32[12,12]{1,0:T(8,128)S(1)} %and_convert_fusion.kept_ref, s32[1]{0:T(128)} %bitcast.1.own_ref, f32[1,12,12,256,256]{4,3,2,1,0:T(8,128)} %place_children.1.sum_ref, f32[3072,1024]{1,0:T(8,128)} %solve_rows.2.solved_ref, ...), custom_call_target="tpu_custom_call", output_to_operand_aliasing={{}: (2, {})} | custom-call | flops 57982058496 | bytes 75497472 | tf_op jit(solution)/shard_map/schur_update/pallas_call | solution.py:199
  (25 shorter events, 0.2 us)
Async XLA Ops:
  6.5 6.9 %copy-start = (f32[1,512,512]{2,1,0:T(8,128)S(1)}, f32[1,512,512]{2,1,0:T(8,128)}, u32[]{:S(2)}) copy-start(f32[1,512,512]{2,1,0:T(8,128)} %param.9) | copy-start | bytes 3145732
  6.5 6.0 %sort.21.cloned.1.call-start = ((), (), s32[]{:S(2)}) async-start(), calls=%async_computation.5 | async-start | bytes 49184 | tf_op jit(solution)/shard_map/jit(argsort)/sort | solution.py:233
  18.7 29.3 %all-to-all-start = ((f32[16,1,16384]{2,1,0:T(1,128)}), f32[16,1,16384]{2,1,0:T(1,128)}, u32[]{:S(2)}, u32[]{:S(2)}) async-start(f32[16,1,16384]{2,1,0:T(1,128)} %bitcast.17), calls=%async_computation | async-start | bytes 2097152 | tf_op jit(solution)/shard_map/all_to_all | solution.py:251
  25.1 70.8 %all-gather.7.cloned.1.call-start = ((), (), s32[]{:S(2)}) async-start(), calls=%async_computation.1 | async-start | bytes 1310720 | tf_op jit(solution)/shard_map/all_gather | solution.py:265
  27.4 2.4 copy-start.10
  49.9 5.6 copy-start.9
  61.5 2.7 copy-start.2
  64.2 208.4 %copy-start.8 = (s32[1,48,48]{2,1,0:T(8,128)S(1)}, s32[1,48,48]{2,1,0:T(8,128)}, u32[]{:S(2)}) copy-start(s32[1,48,48]{2,1,0:T(8,128)} %param.11) | copy-start | bytes 27652
  65.9 64.6 %all-gather.9.cloned.1.call-start = ((), (), s32[]{:S(2)}) async-start(), calls=%async_computation.2 | async-start | bytes 5242880 | tf_op jit(solution)/shard_map/all_gather | solution.py:266
  95.9 356.8 %all-gather.11.cloned.1.call-start = ((), (), s32[]{:S(2)}) async-start(), calls=%async_computation.3 | async-start | bytes 15728640 | tf_op jit(solution)/shard_map/all_gather | solution.py:268
  130.5 368.0 %all-gather.13.cloned.1.call-start = ((), (), s32[]{:S(2)}) async-start(), calls=%async_computation.4 | async-start | bytes 15728640 | tf_op jit(solution)/shard_map/all_gather | solution.py:275
  130.6 141.9 %collective-permute-start = (f32[3072,256]{0,1:T(8,128)}, f32[3072,256]{0,1:T(8,128)}, u32[]{:S(2)}, u32[]{:S(2)}) collective-permute-start(f32[3072,256]{0,1:T(8,128)} %convolution_add_fusion), channel_id=1, source_target_pairs={{0,0},{2,8},{4,16},{6,24},{8,2},{10,10},{12,18},{14,26},{16,4},{18... | collective-permute-start | bytes 9437192 | tf_op jit(solution)/shard_map/ppermute | solution.py:274
  275.3 2.9 copy-start.3
  451.3 1.3 copy-start.5
  465.2 1.6 copy-start.6
  511.1 1.6 copy-start.7
  530.7 2.6 copy-start.4
  533.3 57.1 %copy-start.1 = (f32[1,512,512]{2,1,0:T(8,128)S(1)}, f32[1,512,512]{2,1,0:T(8,128)}, u32[]{:S(2)}) copy-start(f32[1,512,512]{2,1,0:T(8,128)} %param.9) | copy-start | bytes 3145732
Sparse Core Ops, SparseCore 0:
  9.8 2.4 sort.23.cloned.1.call-done
  66.0 29.7 all-gather.6
  97.4 33.0 all-gather.8
  131.9 146.4 all-gather.10
  279.8 218.6 all-gather.12
  (1 shorter events, 0.0 us)
